TPU v7x, 512 devices: a whole 4x8x8 slice. The times are simulated.
512 devices in a mesh: dp: 32 (over z_hi, x, core), mp: 16 (over y, z_lo).
Axes of the slice: x: 4, y: 8, z: 8 (z_hi: 4, z_lo: 2; z = z_hi * 2 + z_lo), core: 2. Of those that a mesh axis runs over, the one named last changes fastest.
Arguments:
- queries: bfloat16 [10240, 6144], P('dp', 'mp'), may hold values from -4.5 to 4.5
- key_rows: bfloat16 [10240, 6144], P('dp', 'mp'), may hold values from -4.5 to 4.5
- value_rows: bfloat16 [10240, 6144], P('dp', 'mp'), may hold values from -6 to 6
- cotangent: bfloat16 [8192, 3072], P('dp'), may hold values from -6 to 6
- out_weight: bfloat16 [6144, 3072], P('mp', 'dp'), may hold values from -0.078125 to 0.078125
- patch_counts: int32 [32, 2], replicated, may hold values from 96 to 160, as said below
- destinations: int32 [32, 2], replicated, may hold values from 0 to 31, as said below
Outputs:
- attended: bfloat16 [8192, 3072], P('dp')
- grad_queries: bfloat16 [10240, 6144], P('dp', 'mp')
- grad_keys: bfloat16 [10240, 6144], P('dp', 'mp')
- grad_values: bfloat16 [10240, 6144], P('dp', 'mp')
- grad_weight: bfloat16 [6144, 3072], P('mp', 'dp')
Inputs may be any that keep to these rules, and one draw needn't show every extreme that they name: `patch_counts`: every image has at most 160 patches; the images assigned to each device have exactly 256 patches in all; in every draw some device holds, in the loader's order, 2 images of 160 patches each. destinations[s, j] = (s - o_j) mod 32, with o_0 drawn afresh each run and o_1 = 31 - o_0; so each device receives one image of each index j.
All inputs are finite; a program needn't handle non-finite values.
Results may differ from a plain program's by a relative error of at most 0.022.
Values may be sent and summed in bfloat16 or wider, within the bound.
A program may use at most 64 MiB of HBM per device.

v0:
```python
import functools
import math

import jax
import jax.numpy as jnp
from jax import lax
from jax.experimental import pallas as pl
from jax.experimental.pallas import tpu as pltpu
from jax.sharding import PartitionSpec as P

HD = 128
HEADS = 3
NDP = 32
SLOT = 160
ROWS = 320
DEST = 256
FEAT = 96
WIDTH = HEADS * HD
OUT = 3072
SUB = DEST // 2
SCALE = 1.0 / math.sqrt(HD)
MESH = pl.DeviceIdType.MESH
F32 = jnp.float32
BF16 = jnp.bfloat16


def dot(a, b, dims):
    return lax.dot_general(a, b, (dims, ((), ())), preferred_element_type=F32)


def place():
    dp = lax.axis_index("dp")
    mp = lax.axis_index("mp")
    return dp, mp, dp // 8, (dp // 2) % 4, dp % 2, mp // 2, mp % 2


def block(i, size):
    return pl.ds(pl.multiple_of(i * size, size), size)


def dp_of(zh, x, core):
    return (zh * 4 + x) * 2 + core


def mod(a, n):
    return lax.rem(a + n, n)


def remote(src, dst, ss, rs, dp, mp):
    return pltpu.make_async_remote_copy(
        src_ref=src, dst_ref=dst, send_sem=ss, recv_sem=rs, device_id=(dp, mp), device_id_type=MESH
    )


def greet(peers):
    barrier = pltpu.get_barrier_semaphore()
    for dp, mp in peers:
        pl.semaphore_signal(barrier, inc=1, device_id=(dp, mp), device_id_type=MESH)


def greeted(count):
    pl.semaphore_wait(pltpu.get_barrier_semaphore(), count)


def tables(counts_ref, dests_ref, dp):
    first = mod(-dests_ref[0, 0], NDP)
    turn = jnp.minimum(first, NDP - 1 - first)
    swap = (first >= NDP // 2).astype(jnp.int32)
    c0 = counts_ref[0, dp]
    c1 = counts_ref[1, dp]
    home = (
        (jnp.where(swap == 1, c0, 0), jnp.where(swap == 1, c1, c0)),
        (jnp.where(swap == 1, 0, c0), jnp.where(swap == 1, c0, c1)),
    )
    src_a = lax.rem(dp + turn, NDP)
    src_b = mod(dp - turn - 1, NDP)
    count_a = counts_ref[swap, src_a]
    count_b = counts_ref[1 - swap, src_b]
    a_first = src_a < src_b
    dest = (
        (jnp.where(a_first, 0, count_b), count_a),
        (jnp.where(a_first, count_a, 0), count_b),
    )
    return home, dest, turn


def iota(shape, dim):
    return lax.broadcasted_iota(jnp.int32, shape, dim)


def pick(rows, start, count):
    shape = (SLOT, rows)
    r, c = iota(shape, 0), iota(shape, 1)
    return jnp.where((c == r + start) & (r < count), 1.0, 0.0).astype(BF16)


def put(rows, start, count):
    shape = (rows, SLOT)
    r, c = iota(shape, 0), iota(shape, 1)
    return jnp.where((r == c + start) & (c < count), 1.0, 0.0).astype(BF16)


def either(slot, pair):
    return [jnp.where(slot == 0, a, b) for a, b in zip(*pair)]


def probabilities(q, k, count):
    scores = dot(q, k, ((1,), (1,))) * SCALE
    scores = jnp.where(iota(scores.shape, 1) < count, scores, -1e30)
    weights = jnp.exp(scores - jnp.max(scores, axis=-1, keepdims=True))
    return weights / jnp.sum(weights, axis=-1, keepdims=True)


def load_rows(refs, qkv_ref, load, first):
    copies = [pltpu.make_async_copy(ref, qkv_ref.at[i], load.at[first + i]) for i, ref in enumerate(refs)]
    for copy in copies:
        copy.start()
    return copies


def pick_rows(rows_ref, qkv_ref, home):
    @pl.loop(0, 6)
    def _(i):
        picked = pick(ROWS, *either(i % 2, home))
        rows_ref[i // 2, i % 2] = dot(picked, qkv_ref[i // 2], ((1,), (0,))).astype(BF16)


def forward_kernel(counts_ref, dests_ref, q_hbm, k_hbm, v_hbm, out_ref, qkv_ref, rows_ref, load):
    home, _, _ = tables(counts_ref, dests_ref, lax.axis_index("dp"))
    for copy in load_rows((q_hbm, k_hbm, v_hbm), qkv_ref, load, 0):
        copy.wait()
    pick_rows(rows_ref, qkv_ref, home)

    @pl.loop(0, 6)
    def _(i):
        slot, cols = i % 2, block(i // 2, HD)
        probs = probabilities(rows_ref[0, slot, :, cols], rows_ref[1, slot, :, cols], either(slot, home)[1])
        out_ref[slot, :, cols] = dot(probs.astype(BF16), rows_ref[2, slot, :, cols], ((1,), (0,))).astype(BF16)


def turn_kernel(turn, in_ref, out_ref, ss, rs):
    dp, mp, *_ = place()
    routes = [(0, mod(dp - turn, NDP)), (1, lax.rem(dp + turn + 1, NDP))]
    others, own = (routes[1:], routes[:1]) if turn == 0 else (routes, [])
    greet([(p, mp) for _, p in others] + [(mod(2 * dp - p, NDP), mp) for _, p in others])
    local = [pltpu.make_async_copy(in_ref.at[i], out_ref.at[i], ss.at[i]) for i, _ in own]
    for copy in local:
        copy.start()
    greeted(2 * len(others))
    copies = [remote(in_ref.at[i], out_ref.at[i], ss.at[i], rs.at[i], p, mp) for i, p in others]
    for copy in copies:
        copy.start()
    for copy in local + copies:
        copy.wait()


def main_kernel(
    counts_ref, dests_ref, turned_ref, q_hbm, k_hbm, v_hbm, cot_hbm, w_hbm,
    att_hbm, gq_hbm, gk_hbm, gv_hbm, gw_hbm,
    qkv_ref, cot_ref, wt_ref, rows_ref, moved_ref, came_ref, dest_ref, part_ref, yring_ref, zring_ref, across_ref,
    half_ref, fold_ref, att_ref, term_ref, core_ref, xin_ref, zin_ref, grads_ref, gw_ref, sum_ref,
    load, store, att_store, wt_s, wt_r, turn_s, turn_r, ring_s, ring_r, fold_s, fold_r, gath_s, gath_r, pass_s, pass_r,
    red_s, red_r,
):
    dp, mp, zh, x, core, y, zl = place()
    up, down = lax.rem(y + 1, 8) * 2 + zl, lax.rem(y + 7, 8) * 2 + zl
    across = y * 2 + 1 - zl
    sibling = dp_of(zh, x, 1 - core)
    xs = [dp_of(zh, lax.rem(x + i, 4), core) for i in (1, 3, 2)]
    zs = [dp_of(lax.rem(zh + i, 4), x, core) for i in (1, 3, 2)]
    peers = [(dp, up), (dp, down), (dp, across)] + [(p, mp) for p in [sibling] + xs + zs]
    peers += [(lax.rem(dp + i, NDP), mp) for i in (1, 2, 4, 8, 24, 28, 30, 31)]
    greet(peers)

    loads = [pltpu.make_async_copy(w_hbm, wt_ref.at[dp], load.at[0]), pltpu.make_async_copy(cot_hbm, cot_ref, load.at[1])]
    for copy in loads:
        copy.start()
    loads += load_rows((q_hbm, k_hbm, v_hbm), qkv_ref, load, 2)
    home, dest, turn = tables(counts_ref, dests_ref, dp)
    pending = []

    def shard_send(i, shard, to):
        remote(wt_ref.at[shard], wt_ref.at[shard], wt_s.at[i], wt_r.at[shard], to, mp).start()

    def shard_wait(shard):
        remote(wt_ref.at[shard], wt_ref.at[shard], wt_s.at[0], wt_r.at[shard], dp, mp).wait_recv()

    def shard_sent(i):
        remote(wt_ref.at[dp], wt_ref.at[dp], wt_s.at[i], wt_r.at[dp], sibling, mp).wait_send()

    odd = lax.rem(y, 2)
    order = [lax.rem((y + 4) // 2 + i, 4) for i in (0, 3 - 2 * odd, 1 + 2 * odd, 2)]

    def z_arrive(i):
        @pl.when(order[i] != zh)
        def _():
            shard = dp_of(order[i], x, core)
            shard_wait(shard)
            for j, p in enumerate(xs + [sibling]):
                shard_send(7 + 4 * i + j, shard, p)

    def x_arrive(i):
        for j in range(3):
            shard = dp_of(order[i], lax.rem(x + (1, 3, 2)[j], 4), core)
            shard_wait(shard)
            shard_send(23 + 3 * i + j, shard, sibling)
        for j in range(4):
            shard_wait(dp_of(order[i], j, 1 - core))

    def partial(i):
        for j in range(2):
            c = 2 * order[i] + j
            w = wt_ref[pl.ds(4 * c, 4)].reshape(WIDTH, WIDTH)
            part_ref[lax.rem(c - y + 8, 8)] = dot(dest_ref[...], w, ((1,), (1,))).astype(BF16)

    loads[0].wait()
    greeted(len(peers))
    for i, p in enumerate(zs + xs + [sibling]):
        shard_send(i, dp, p)

    def place_rows(ref, parts, spans):
        @pl.loop(0, ref.shape[0] // 64)
        def _(i):
            rows = 0.0
            for part, (start, count) in zip(parts, spans):
                rows = rows + dot(put(64, start - 64 * i, count), part[...], ((1,), (0,)))
            ref[block(i, 64)] = rows.astype(BF16)

    place_rows(dest_ref, [turned_ref.at[0], turned_ref.at[1]], dest)
    loads[1].wait()

    @pl.loop(0, 8)
    def _(c):
        term = dot(cot_ref[:, block(c, WIDTH)], dest_ref[...], ((0,), (0,))).astype(BF16)
        for i in range(4):
            term_ref[i % 2, lax.rem(2 * c + i // 2, 4), c // 2] = term[i * FEAT : (i + 1) * FEAT]

    for i in range(4):
        z_arrive(i)
    swap = remote(term_ref.at[1 - core], core_ref, red_s.at[0], red_r.at[0], sibling, mp)
    swap.start()
    pending.append(swap)
    for i in range(2):
        x_arrive(i)

    mine, other = pl.ds(pl.multiple_of(64 * zl, 64), 64), pl.ds(pl.multiple_of(64 - 64 * zl, 64), 64)
    low_mine = pl.ds(pl.multiple_of(SUB + 64 * zl, 64), 64)
    low_other = pl.ds(pl.multiple_of(SUB + 64 - 64 * zl, 64), 64)

    def ring_copy(zone, way, step):
        c = 4 - step if way == 0 else 4 + step
        src = half_ref.at[c] if zone else part_ref.at[c, pl.ds(0, SUB)]
        dst = (zring_ref if zone else yring_ref).at[way, step]
        sem = (zone, way, step)
        return remote(src, dst, ring_s.at[sem], ring_r.at[sem], dp, up if way == 0 else down)

    def ring_send(zone, way, step):
        ring_copy(zone, way, step).start()

    def ring_take(zone, way, step):
        ring_copy(zone, way, step).wait_recv()
        c = 3 - step if way == 0 else 5 + step
        ref = half_ref.at[c] if zone else part_ref.at[c, pl.ds(0, SUB)]
        add(ref, ref, (zring_ref if zone else yring_ref).at[way, step])

    def add(out, *refs):
        @pl.loop(0, out.shape[0] // 32)
        def _(i):
            total = 0.0
            for ref in refs:
                total = total + ref[block(i, 32)].astype(F32)
            out[block(i, 32)] = total.astype(BF16)

    shares = []

    def share_send(lo, hi):
        i, span = len(shares), pl.ds(lo, hi - lo)
        copy = remote(part_ref.at[span, low_other], across_ref.at[span], fold_s.at[i], fold_r.at[i], dp, across)
        copy.start()
        shares.append((copy, lo, hi))
        pending.append(copy)

    def share_take(i):
        copy, lo, hi = shares[i]
        copy.wait_recv()

        @pl.loop(lo, hi)
        def _(c):
            add(half_ref.at[c], part_ref.at[c, low_mine], across_ref.at[c])

    partial(0)
    partial(1)
    ring_send(0, 0, 0)
    ring_send(0, 1, 1)
    share_send(3, 6)
    x_arrive(2)
    partial(2)
    share_take(0)
    ring_send(1, 1, 0)
    ring_send(1, 0, 1)
    x_arrive(3)
    partial(3)
    share_send(0, 3)
    share_send(6, 8)
    ring_take(0, 0, 0)
    ring_send(0, 0, 1)

    sum_ref[...] = jnp.zeros_like(sum_ref)

    @pl.loop(0, 8)
    def _(c):
        w = wt_ref[pl.ds(4 * c, 4)].reshape(WIDTH, WIDTH)
        sum_ref[...] += dot(cot_ref[:, block(c, WIDTH)], w, ((1,), (0,)))

    moved_ref[1, 0] = dot(pick(DEST, *dest[0]), sum_ref[...].astype(BF16), ((1,), (0,))).astype(BF16)
    moved_ref[0, 1] = dot(pick(DEST, *dest[1]), sum_ref[...].astype(BF16), ((1,), (0,))).astype(BF16)

    def shift_copy(i, slot):
        by = (1, 8, 4, 2, 1)[i]
        to = mod(dp - by, NDP) if slot else lax.rem(dp + by, NDP)
        dst = came_ref.at[i, slot] if i else moved_ref.at[1, 1]
        return remote(moved_ref.at[i, slot], dst, turn_s.at[i, slot], turn_r.at[i, slot], to, mp)

    def shift_send(i):
        for slot in range(0 if i else 1, 2):
            shift_copy(i, slot).start()
            pending.append(shift_copy(i, slot))

    def shift_take(i):
        for slot in range(0 if i else 1, 2):
            shift_copy(i, slot).wait_recv()
            if i:
                taken = lax.rem(turn // (1, 8, 4, 2, 1)[i], 2) == 1
                moved_ref[i + 1, slot] = jnp.where(taken, came_ref[i, slot], moved_ref[i, slot])

    shift_send(0)

    swap.wait_recv()
    @pl.loop(0, 16)
    def _(i):
        ref = term_ref.at[core, i // 4, lax.rem(i, 4)]
        add(ref, ref, core_ref.at[i // 4, lax.rem(i, 4)])

    xcopies = []
    for n, i in enumerate((1, 3, 2)):
        copy = remote(term_ref.at[core, lax.rem(x + i, 4)], xin_ref.at[n], red_s.at[1 + n], red_r.at[1 + n], xs[n], mp)
        copy.start()
        xcopies.append(copy)
    pending.extend(xcopies)

    share_take(1)
    share_take(2)
    ring_take(1, 1, 0)
    ring_send(1, 1, 1)
    shift_take(0)
    shift_send(1)
    for step in (1, 2):
        for zone, way in ((0, 1), (1, 0), (0, 0), (1, 1)):
            ring_take(zone, way, step)
            ring_send(zone, way, step + 1)
    shift_take(1)
    shift_send(2)
    loads[2].wait()
    loads[3].wait()
    loads[4].wait()
    pick_rows(rows_ref, qkv_ref, home)

    for way in range(2):
        ring_copy(0, way, 3).wait_recv()
    own = part_ref.at[0, pl.ds(0, SUB)]
    add(own, own, yring_ref.at[0, 3], yring_ref.at[1, 3])
    fold = remote(part_ref.at[0, other], fold_ref, fold_s.at[3], fold_r.at[3], dp, across)
    fold.start()
    for way in range(2):
        ring_copy(1, way, 3).wait_recv()
    add(att_ref.at[0, low_mine], half_ref.at[0], zring_ref.at[0, 3], zring_ref.at[1, 3])

    def low_copy(rows):
        return remote(att_ref.at[0, rows], att_ref.at[0, rows], fold_s.at[4], fold_r.at[4], dp, across)

    low_copy(low_mine).start()
    pending.extend([fold, low_copy(low_mine)])

    def att_copy(zone, c):
        rows, cols = pl.ds(zone * SUB, SUB), block(lax.rem(y + c, 8), WIDTH)
        return pltpu.make_async_copy(att_ref.at[c, rows], att_hbm.at[rows, cols], att_store.at[zone, c])

    def gather_copy(zone, way, step):
        rows = pl.ds(SUB, SUB) if zone else mine
        src, dst = (lax.rem(8 - step, 8), 7 - step) if way == 0 else (step, step + 1)
        sem = (zone, way, step)
        return remote(
            att_ref.at[src, rows], att_ref.at[dst, rows], gath_s.at[sem], gath_r.at[sem], dp, up if way == 0 else down
        )

    def gather_send(zone, way, step):
        gather_copy(zone, way, step).start()

    def pass_copy(c, rows):
        return remote(att_ref.at[c, rows], att_ref.at[c, rows], pass_s.at[c], pass_r.at[c], dp, across)

    def gather_take(zone, way, step):
        gather_copy(zone, way, step).wait_recv()
        c = 7 - step if way == 0 else step + 1
        if zone:
            att_copy(1, c).start()
        else:
            pass_copy(c, mine).start()

    fold.wait_recv()
    add(att_ref.at[0, mine], part_ref.at[0, mine], fold_ref)
    gather_send(0, 0, 0)
    gather_send(0, 1, 0)
    pass_copy(0, mine).start()
    low_copy(low_other).wait_recv()
    gather_send(1, 0, 0)
    gather_send(1, 1, 0)
    att_copy(1, 0).start()

    for copy in xcopies:
        copy.wait_recv()

    @pl.loop(0, 4)
    def _(i):
        add(term_ref.at[core, x, i], term_ref.at[core, x, i], *[xin_ref.at[n, i] for n in range(3)])

    zcopies = []
    for n, i in enumerate((1, 3, 2)):
        copy = remote(
            term_ref.at[core, x, lax.rem(zh + i, 4)], zin_ref.at[n], red_s.at[4 + n], red_r.at[4 + n], zs[n], mp
        )
        copy.start()
        zcopies.append(copy)
    pending.extend(zcopies)

    outs = []
    shift_take(2)
    shift_send(3)
    for step in range(2):
        for zone, way in ((0, 0), (0, 1), (1, 0), (1, 1)):
            gather_take(zone, way, step)
            gather_send(zone, way, step + 1)
        shift_take(3 + step)
        if step == 0:
            shift_send(4)

    @pl.loop(0, 6)
    def _(i):
        slot, cols = i % 2, block(i // 2, HD)
        q, k, v = rows_ref[0, slot, :, cols], rows_ref[1, slot, :, cols], rows_ref[2, slot, :, cols]
        gm = moved_ref[5, slot, :, cols]
        probs = probabilities(q, k, either(slot, home)[1])
        gp = dot(gm, v, ((1,), (1,)))
        inner = jnp.sum(gp * probs, axis=-1, keepdims=True)
        gs = (probs * (gp - inner) * SCALE).astype(BF16)
        rows_ref[0, slot, :, cols] = dot(gs, k, ((1,), (0,))).astype(BF16)
        rows_ref[1, slot, :, cols] = dot(gs, q, ((0,), (0,))).astype(BF16)
        rows_ref[2, slot, :, cols] = dot(probs.astype(BF16), gm, ((0,), (0,))).astype(BF16)

    @pl.loop(0, 3)
    def _(i):
        place_rows(grads_ref.at[i], [rows_ref.at[i, 0], rows_ref.at[i, 1]], home)

    for i, ref in enumerate((gq_hbm, gk_hbm, gv_hbm)):
        outs.append(pltpu.make_async_copy(grads_ref.at[i], ref, store.at[i]))
    for copy in outs:
        copy.start()

    for zone, way in ((0, 1), (1, 0), (0, 0), (1, 1)):
        gather_take(zone, way, 2)
        if zone != way:
            gather_send(zone, way, 3)
    for copy in zcopies:
        copy.wait_recv()
    add(gw_ref, term_ref.at[core, x, zh], *[zin_ref.at[n] for n in range(3)])
    outs.append(pltpu.make_async_copy(gw_ref, gw_hbm, store.at[3]))
    outs[-1].start()
    gather_take(0, 1, 3)
    gather_take(1, 0, 3)

    @pl.loop(0, 8)
    def _(c):
        pass_copy(c, other).wait_recv()
        att_copy(0, c).start()

    for copy in outs:
        copy.wait()

    @pl.loop(0, 8)
    def _(c):
        att_copy(0, c).wait()
        att_copy(1, c).wait()
        pass_copy(c, mine).wait_send()

    for zone in range(2):
        for way in range(2):
            @pl.loop(0 if zone == way else 1, 4)
            def _(step):
                ring_copy(zone, way, step).wait_send()

            @pl.loop(0, 3 if zone == way else 4)
            def _(step):
                gather_copy(zone, way, step).wait_send()

    for i in range(4):

        @pl.when(order[i] != zh)
        def _():
            for j in range(4):
                shard_sent(7 + 4 * i + j)

    for i in [*range(7), *range(23, 35)]:
        shard_sent(i)
    for copy in pending:
        copy.wait_send()


def sds(*shape):
    return jax.ShapeDtypeStruct(shape, BF16)


def buf(*shape):
    return pltpu.VMEM(shape, BF16)


DMA = pltpu.SemaphoreType.DMA


def local(queries, key_rows, value_rows, cotangent, out_weight, patch_counts, destinations):
    smem, hbm, vmem = [pl.BlockSpec(memory_space=space) for space in (pltpu.SMEM, pl.ANY, pltpu.VMEM)]
    counts, dests = patch_counts.T, destinations.T
    mixed = pl.pallas_call(
        forward_kernel,
        out_shape=sds(2, SLOT, WIDTH),
        in_specs=[smem, smem] + [hbm] * 3,
        out_specs=vmem,
        scratch_shapes=[buf(3, ROWS, WIDTH), buf(3, 2, SLOT, WIDTH), DMA((3,))],
        compiler_params=pltpu.CompilerParams(vmem_limit_bytes=32 << 20),
        name="forward",
    )(counts, dests, queries, key_rows, value_rows)

    def branch(turn):
        return pl.pallas_call(
            functools.partial(turn_kernel, turn),
            out_shape=sds(2, SLOT, WIDTH),
            in_specs=[vmem],
            out_specs=vmem,
            scratch_shapes=[DMA((2,)), DMA((2,))],
            compiler_params=pltpu.CompilerParams(collective_id=1 + turn, has_side_effects=True),
            name="turn_%d" % turn,
        )

    first = -destinations[0, 0] & (NDP - 1)
    index = jnp.minimum(first, NDP - 1 - first)
    turned = lax.switch(index, [branch(turn) for turn in range(NDP // 2)], mixed)

    *outs, grad_weight = pl.pallas_call(
        main_kernel,
        out_shape=(sds(DEST, OUT), sds(ROWS, WIDTH), sds(ROWS, WIDTH), sds(ROWS, WIDTH), sds(FEAT, WIDTH)),
        in_specs=[smem, smem, vmem] + [hbm] * 5,
        out_specs=(hbm,) * 5,
        scratch_shapes=[
            buf(3, ROWS, WIDTH), buf(DEST, OUT), buf(NDP, FEAT, WIDTH), buf(3, 2, SLOT, WIDTH),
            buf(6, 2, SLOT, WIDTH), buf(5, 2, SLOT, WIDTH), buf(DEST, WIDTH), buf(8, DEST, WIDTH),
            buf(2, 4, SUB, WIDTH), buf(2, 4, 64, WIDTH), buf(8, 64, WIDTH), buf(8, 64, WIDTH), buf(64, WIDTH),
            buf(8, DEST, WIDTH), buf(2, 4, 4, FEAT, WIDTH), buf(4, 4, FEAT, WIDTH), buf(3, 4, FEAT, WIDTH),
            buf(3, FEAT, WIDTH), buf(3, ROWS, WIDTH), buf(FEAT, WIDTH), pltpu.VMEM((DEST, WIDTH), F32),
            DMA((5,)), DMA((4,)), DMA((2, 8)), DMA((35,)), DMA((NDP,)), DMA((5, 2)), DMA((5, 2)),
            DMA((2, 2, 4)), DMA((2, 2, 4)), DMA((5,)), DMA((5,)), DMA((2, 2, 4)), DMA((2, 2, 4)),
            DMA((8,)), DMA((8,)), DMA((7,)), DMA((7,)),
        ],
        compiler_params=pltpu.CompilerParams(collective_id=0, has_side_effects=True, vmem_limit_bytes=40 << 20),
        name="project_backward",
    )(counts, dests, turned, queries, key_rows, value_rows, cotangent, out_weight.T)
    return (*outs, grad_weight.T)


def solution(mesh):
    in_specs = (P("dp", "mp"), P("dp", "mp"), P("dp", "mp"), P("dp", None), P("mp", "dp"), P(), P())
    out_specs = (P("dp", None), P("dp", "mp"), P("dp", "mp"), P("dp", "mp"), P("mp", "dp"))
    return jax.shard_map(local, mesh=mesh, in_specs=in_specs, out_specs=out_specs, check_vma=False)
```

profile of v0, /device:TPU:80, one launch (start us, length us, event | category | flops | bytes accessed | tf_op | source)
XLA Modules:
  0.0 135.7 jit_solution(18083219953717526122)
XLA Ops:
  0.6 1.2 slice.3
  2.5 0.0 copy-start.1
  2.5 0.9 copy-done.1
  3.4 0.0 copy-start.3
  3.4 0.9 copy-done.3
  4.4 0.0 copy-start.5
  4.4 0.9 copy-done.5
  5.3 0.0 copy-start.8
  5.3 0.7 copy-done.8
  6.0 0.0 copy-start.10
  6.0 0.7 copy-done.10
  6.7 5.9 %forward.1 = bf16[2,160,384]{2,1,0:T(8,128)(2,1)S(1)} custom-call(s32[2,32]{1,0:T(2,128)S(1)} %bitcast.7, s32[2,32]{1,0:T(2,128)S(1)} %bitcast.9, bf16[320,384]{1,0:T(8,128)(2,1)S(1)} %copy-done.1, bf16[320,384]{1,0:T(8,128)(2,1)S(1)} %copy-done.3, bf16[320,384]{1,0:T(8,128)(2,1)S(1)} %copy-done.5), custom_call_target="tpu_custom_call" | custom-call | tf_op jit(solution)/shard_map/forward/pallas_call | solution.py:532
  12.5 0.0 copy-start
  12.6 0.0 copy-start.2
  12.6 0.0 copy-start.4
  12.6 0.0 copy-start.6
  12.6 0.0 copy-start.7
  12.6 0.0 copy-start.9
  12.6 0.0 copy-start.11
  12.6 20.5 %conditional.1 = (bf16[2,160,384]{2,1,0:T(8,128)(2,1)S(1)}) conditional(s32[]{:T(128)} %clamp.3, bf16[2,160,384]{2,1,0:T(8,128)(2,1)S(1)} %forward.1, bf16[2,160,384]{2,1,0:T(8,128)(2,1)S(1)} %forward.1, bf16[2,160,384]{2,1,0:T(8,128)(2,1)S(1)} %forward.1, bf16[2,160,384]{2,1,0:T(8,128)(2,1)S(1)} %forward.1, ...), branch_computations={%region_0.0_spmd, %region_1.0_spmd, %region_2.0_spmd, %region_3.0_... | conditional | bytes 8 | solution.py:555
  12.7 20.4 %turn_15.1 = bf16[2,160,384]{2,1,0:T(8,128)(2,1)S(1)} custom-call(bf16[2,160,384]{2,1,0:T(8,128)(2,1)S(1)} %in_ref.15), custom_call_target="tpu_custom_call" | custom-call | tf_op jit(solution)/shard_map/cond/branch_15_fun/turn_15/pallas_call | solution.py:555
  33.1 0.0 copy-done
  33.1 0.0 copy-done.2
  33.1 0.0 copy-done.4
  33.1 0.0 copy-done.6
  33.2 0.0 copy-done.7
  33.2 0.0 copy-done.9
  33.2 0.0 copy-done.11
  33.2 98.7 %project_backward.1 = (bf16[256,3072]{1,0:T(8,128)(2,1)S(1)}, bf16[320,384]{1,0:T(8,128)(2,1)S(1)}, bf16[320,384]{1,0:T(8,128)(2,1)S(1)}, bf16[320,384]{1,0:T(8,128)(2,1)S(1)}, bf16[96,384]{1,0:T(8,128)(2,1)S(1)}) custom-call(s32[2,32]{1,0:T(2,128)S(1)} %bitcast.8, s32[2,32]{1,0:T(2,128)S(1)} %bitcast.10, ...), custom_call_target="tpu_custom_call" | custom-call | tf_op jit(solution)/shard_map/project_backward/pallas_call | solution.py:557
  131.8 1.1 copy.33
  133.0 0.7 copy.34
  133.7 0.7 copy.35
  134.4 0.7 copy.36
  135.1 0.6 copy.37
Async XLA Ops:
  2.5 0.9 copy-start.1
  3.4 0.9 copy-start.3
  4.4 0.9 copy-start.5
  5.3 0.7 copy-start.8
  6.0 0.7 copy-start.10
  12.5 20.6 %copy-start = (bf16[256,3072]{1,0:T(8,128)(2,1)S(1)}, bf16[256,3072]{1,0:T(8,128)(2,1)}, u32[]{:S(2)}) copy-start(bf16[256,3072]{1,0:T(8,128)(2,1)} %cot_hbm.1) | copy-start | bytes 4718596
  12.6 20.6 %copy-start.2 = (bf16[320,384]{1,0:T(8,128)(2,1)S(1)}, bf16[320,384]{1,0:T(8,128)(2,1)}, u32[]{:S(2)}) copy-start(bf16[320,384]{1,0:T(8,128)(2,1)} %q_hbm.3) | copy-start | bytes 737284
  12.6 20.6 %copy-start.4 = (bf16[320,384]{1,0:T(8,128)(2,1)S(1)}, bf16[320,384]{1,0:T(8,128)(2,1)}, u32[]{:S(2)}) copy-start(bf16[320,384]{1,0:T(8,128)(2,1)} %k_hbm.3) | copy-start | bytes 737284
  12.6 20.6 %copy-start.6 = (bf16[320,384]{1,0:T(8,128)(2,1)S(1)}, bf16[320,384]{1,0:T(8,128)(2,1)}, u32[]{:S(2)}) copy-start(bf16[320,384]{1,0:T(8,128)(2,1)} %v_hbm.3) | copy-start | bytes 737284
  12.6 20.6 %copy-start.7 = (bf16[384,96]{0,1:T(8,128)(2,1)S(1)}, bf16[384,96]{0,1:T(8,128)(2,1)}, u32[]{:S(2)}) copy-start(bf16[384,96]{0,1:T(8,128)(2,1)} %param.27) | copy-start | bytes 221188
  12.6 20.6 %copy-start.9 = (s32[32,2]{0,1:T(2,128)S(1)}, s32[32,2]{0,1:T(2,128)}, u32[]{:S(2)}) copy-start(s32[32,2]{0,1:T(2,128)} %param.28) | copy-start | bytes 772
  12.6 20.6 %copy-start.11 = (s32[32,2]{0,1:T(2,128)S(1)}, s32[32,2]{0,1:T(2,128)}, u32[]{:S(2)}) copy-start(s32[32,2]{0,1:T(2,128)} %param.29) | copy-start | bytes 772
where the time goes:
time: 136 us
  Pallas kernels  125 us (92%)
  local copies, waits for them, and re-layouts  9.27 us (7%)
  between operations  1.44 us (1%)
    pallas_call x1, Pallas kernels, local(): pl.pallas_call(main_kernel, out_shape=(sds(DEST, OUT), sds(ROWS, WIDTH),...  98.7 us
    pallas_call x1, Pallas kernels, local(): lax.switch(index, [branch(turn) for turn in range(NDP // 2)], mixed)  20.4 us
    unnamed x29, local copies, waits for them, and re-layouts  8.08 us
    pallas_call x1, Pallas kernels, local(): pl.pallas_call(forward_kernel, out_shape=sds(2, SLOT, WIDTH), in_specs=[s...  5.86 us

commit v1 on v0

v1 whole, which is shorter than its diff:
```python
import functools
import math

import jax
import jax.numpy as jnp
from jax import lax
from jax.experimental import pallas as pl
from jax.experimental.pallas import tpu as pltpu
from jax.sharding import PartitionSpec as P

HD = 128
HEADS = 3
NDP = 32
SLOT = 160
ROWS = 320
DEST = 256
FEAT = 96
WIDTH = HEADS * HD
OUT = 3072
SUB = DEST // 2
SCALE = 1.0 / math.sqrt(HD)
MESH = pl.DeviceIdType.MESH
F32 = jnp.float32
BF16 = jnp.bfloat16


def dot(a, b, dims):
    return lax.dot_general(a, b, (dims, ((), ())), preferred_element_type=F32)


def place():
    dp = lax.axis_index("dp")
    mp = lax.axis_index("mp")
    return dp, mp, dp // 8, (dp // 2) % 4, dp % 2, mp // 2, mp % 2


def block(i, size):
    return pl.ds(pl.multiple_of(i * size, size), size)


def dp_of(zh, x, core):
    return (zh * 4 + x) * 2 + core


def mod(a, n):
    return lax.rem(a + n, n)


def remote(src, dst, ss, rs, dp, mp):
    return pltpu.make_async_remote_copy(
        src_ref=src, dst_ref=dst, send_sem=ss, recv_sem=rs, device_id=(dp, mp), device_id_type=MESH
    )


def greet(peers):
    barrier = pltpu.get_barrier_semaphore()
    for dp, mp in peers:
        pl.semaphore_signal(barrier, inc=1, device_id=(dp, mp), device_id_type=MESH)


def greeted(count):
    pl.semaphore_wait(pltpu.get_barrier_semaphore(), count)


def tables(counts_ref, dests_ref, dp):
    first = mod(-dests_ref[0, 0], NDP)
    turn = jnp.minimum(first, NDP - 1 - first)
    swap = (first >= NDP // 2).astype(jnp.int32)
    c0 = counts_ref[0, dp]
    c1 = counts_ref[1, dp]
    home = (
        (jnp.where(swap == 1, c0, 0), jnp.where(swap == 1, c1, c0)),
        (jnp.where(swap == 1, 0, c0), jnp.where(swap == 1, c0, c1)),
    )
    src_a = lax.rem(dp + turn, NDP)
    src_b = mod(dp - turn - 1, NDP)
    count_a = counts_ref[swap, src_a]
    count_b = counts_ref[1 - swap, src_b]
    a_first = src_a < src_b
    dest = (
        (jnp.where(a_first, 0, count_b), count_a),
        (jnp.where(a_first, count_a, 0), count_b),
    )
    return home, dest, turn


def iota(shape, dim):
    return lax.broadcasted_iota(jnp.int32, shape, dim)


def pick(rows, start, count):
    shape = (SLOT, rows)
    r, c = iota(shape, 0), iota(shape, 1)
    return jnp.where((c == r + start) & (r < count), 1.0, 0.0).astype(BF16)


def put(rows, start, count):
    shape = (rows, SLOT)
    r, c = iota(shape, 0), iota(shape, 1)
    return jnp.where((r == c + start) & (c < count), 1.0, 0.0).astype(BF16)


def either(slot, pair):
    return [jnp.where(slot == 0, a, b) for a, b in zip(*pair)]


def probabilities(q, k, count):
    scores = dot(q, k, ((1,), (1,))) * SCALE
    scores = jnp.where(iota(scores.shape, 1) < count, scores, -1e30)
    weights = jnp.exp(scores - jnp.max(scores, axis=-1, keepdims=True))
    return weights / jnp.sum(weights, axis=-1, keepdims=True)


def load_rows(refs, qkv_ref, load, first):
    copies = [pltpu.make_async_copy(ref, qkv_ref.at[i], load.at[first + i]) for i, ref in enumerate(refs)]
    for copy in copies:
        copy.start()
    return copies


def pick_rows(rows_ref, qkv_ref, home):
    @pl.loop(0, 6)
    def _(i):
        picked = pick(ROWS, *either(i % 2, home))
        rows_ref[i // 2, i % 2] = dot(picked, qkv_ref[i // 2], ((1,), (0,))).astype(BF16)


def add(out, *refs):
    @pl.loop(0, out.shape[0] // 32)
    def _(i):
        total = 0.0
        for ref in refs:
            total = total + ref[block(i, 32)].astype(F32)
        out[block(i, 32)] = total.astype(BF16)


def place_rows(ref, parts, spans):
    @pl.loop(0, ref.shape[0] // 64)
    def _(i):
        rows = 0.0
        for part, (start, count) in zip(parts, spans):
            rows = rows + dot(put(64, start - 64 * i, count), part[...], ((1,), (0,)))
        ref[block(i, 64)] = rows.astype(BF16)


def gather_kernel(
    counts_ref, dests_ref, q_hbm, k_hbm, v_hbm, cot_hbm, w_hbm, slots_ref, wt_hbm,
    qkv_ref, cot_ref, wt_ref, rows_ref, sum_ref, load, store, wt_s, wt_r,
):
    dp, mp, zh, x, core, *_ = place()
    sibling = dp_of(zh, x, 1 - core)
    xs = [dp_of(zh, lax.rem(x + i, 4), core) for i in (1, 3, 2)]
    zs = [dp_of(lax.rem(zh + i, 4), x, core) for i in (1, 3, 2)]
    greet([(p, mp) for p in [sibling] + xs + zs])
    loads = [pltpu.make_async_copy(w_hbm, wt_ref.at[dp], load.at[0]), pltpu.make_async_copy(cot_hbm, cot_ref, load.at[1])]
    loads[0].start()
    loads += load_rows((q_hbm, k_hbm, v_hbm), qkv_ref, load, 2)
    loads[1].start()
    home, dest, _ = tables(counts_ref, dests_ref, dp)

    def shard_copy(i, shard, to):
        return remote(wt_ref.at[shard], wt_ref.at[shard], wt_s.at[i], wt_r.at[shard], to, mp)

    loads[0].wait()
    greeted(7)
    for i, p in enumerate(zs + xs + [sibling]):
        shard_copy(i, dp, p).start()

    for copy in loads[2:]:
        copy.wait()
    pick_rows(rows_ref, qkv_ref, home)

    @pl.loop(0, 6)
    def _(i):
        slot, cols = i % 2, block(i // 2, HD)
        probs = probabilities(rows_ref[0, slot, :, cols], rows_ref[1, slot, :, cols], either(slot, home)[1])
        slots_ref[slot, :, cols] = dot(probs.astype(BF16), rows_ref[2, slot, :, cols], ((1,), (0,))).astype(BF16)

    for i in range(3):
        shard_copy(0, zs[i], dp).wait_recv()
        for j, p in enumerate(xs + [sibling]):
            shard_copy(7 + 4 * i + j, zs[i], p).start()
    for i in range(4):
        for j in range(3):
            shard = dp_of(lax.rem(zh + (0, 1, 3, 2)[i], 4), lax.rem(x + (1, 3, 2)[j], 4), core)
            shard_copy(0, shard, dp).wait_recv()
            shard_copy(19 + 3 * i + j, shard, sibling).start()

    @pl.loop(0, 16)
    def _(i):
        shard_copy(0, 2 * i + 1 - core, dp).wait_recv()

    store_wt = pltpu.make_async_copy(wt_ref, wt_hbm, store.at[0])
    store_wt.start()
    loads[1].wait()
    sum_ref[...] = jnp.zeros_like(sum_ref)

    @pl.loop(0, 8)
    def _(c):
        w = wt_ref[pl.ds(4 * c, 4)].reshape(WIDTH, WIDTH)
        sum_ref[...] += dot(cot_ref[:, block(c, WIDTH)], w, ((1,), (0,)))

    for slot in range(2):
        slots_ref[2 + slot] = dot(pick(DEST, *dest[slot]), sum_ref[...].astype(BF16), ((1,), (0,))).astype(BF16)

    @pl.loop(0, 31)
    def _(i):
        shard_copy(i, dp, sibling).wait_send()

    store_wt.wait()


def turn_kernel(turn, in_ref, out_ref, ss, rs):
    dp, mp, *_ = place()
    back_a, on_a = mod(dp - turn, NDP), lax.rem(dp + turn, NDP)
    on_b, back_b = lax.rem(dp + turn + 1, NDP), mod(dp - turn - 1, NDP)
    routes = [(0, back_a), (1, on_b), (2, on_a), (3, back_b)]
    others, own = (routes[1::2], routes[::2]) if turn == 0 else (routes, [])
    greet([(p, mp) for _, p in others])
    local = [pltpu.make_async_copy(in_ref.at[i], out_ref.at[i], ss.at[i]) for i, _ in own]
    for copy in local:
        copy.start()
    greeted(len(others))
    copies = [remote(in_ref.at[i], out_ref.at[i], ss.at[i], rs.at[i], p, mp) for i, p in others]
    for copy in copies:
        copy.start()
    for copy in local + copies:
        copy.wait()


def main_kernel(
    counts_ref, dests_ref, turned_ref, q_hbm, k_hbm, v_hbm, cot_hbm, wt_hbm,
    att_hbm, gq_hbm, gk_hbm, gv_hbm, gw_hbm,
    qkv_ref, cot_ref, wt_ref, rows_ref, dest_ref, part_ref, ring_ref, across_ref, half_ref, fold_ref, att_ref,
    term_ref, core_ref, xin_ref, zin_ref, grads_ref, gw_ref,
    load, store, att_store, ring_s, ring_r, fold_s, fold_r, gath_s, gath_r, pass_s, pass_r, red_s, red_r,
):
    dp, mp, zh, x, core, y, zl = place()
    up, down = lax.rem(y + 1, 8) * 2 + zl, lax.rem(y + 7, 8) * 2 + zl
    across = y * 2 + 1 - zl
    sibling = dp_of(zh, x, 1 - core)
    xs = [dp_of(zh, lax.rem(x + i, 4), core) for i in (1, 3, 2)]
    zs = [dp_of(lax.rem(zh + i, 4), x, core) for i in (1, 3, 2)]
    greet([(dp, up), (dp, down), (dp, across)] + [(p, mp) for p in [sibling] + xs + zs])
    loads = [pltpu.make_async_copy(wt_hbm, wt_ref, load.at[0]), pltpu.make_async_copy(cot_hbm, cot_ref, load.at[1])]
    for copy in loads:
        copy.start()
    loads += load_rows((q_hbm, k_hbm, v_hbm), qkv_ref, load, 2)
    home, dest, _ = tables(counts_ref, dests_ref, dp)
    place_rows(dest_ref, [turned_ref.at[0], turned_ref.at[1]], dest)
    pending = []

    mine, other = pl.ds(pl.multiple_of(64 * zl, 64), 64), pl.ds(pl.multiple_of(64 - 64 * zl, 64), 64)
    low_mine = pl.ds(pl.multiple_of(SUB + 64 * zl, 64), 64)
    low_other = pl.ds(pl.multiple_of(SUB + 64 - 64 * zl, 64), 64)

    def ring_ref_of(zone, c):
        return half_ref.at[c] if zone == 2 else part_ref.at[c, pl.ds(64 * zone, 64)]

    def ring_copy(zone, way, step):
        c = 4 - step if way == 0 else 4 + step
        sem = (zone, way, step)
        return remote(ring_ref_of(zone, c), ring_ref.at[sem], ring_s.at[sem], ring_r.at[sem], dp, (up, down)[way])

    def ring_send(zone, way, step):
        copy = ring_copy(zone, way, step)
        copy.start()
        pending.append(copy)

    def ring_take(zone, way, step):
        ring_copy(zone, way, step).wait_recv()
        ref = ring_ref_of(zone, 3 - step if way == 0 else 5 + step)
        add(ref, ref, ring_ref.at[zone, way, step])

    def partial(c):
        w = wt_ref[pl.ds(4 * lax.rem(y + c, 8), 4)].reshape(WIDTH, WIDTH)
        part_ref[c] = dot(dest_ref[...], w, ((1,), (1,))).astype(BF16)

    shares = []

    def share_send(lo, hi):
        i, span = len(shares), pl.ds(lo, hi - lo)
        copy = remote(part_ref.at[span, low_other], across_ref.at[span], fold_s.at[i], fold_r.at[i], dp, across)
        copy.start()
        shares.append((copy, lo, hi))
        pending.append(copy)

    def share_take(i):
        copy, lo, hi = shares[i]
        copy.wait_recv()

        @pl.loop(lo, hi)
        def _(c):
            add(half_ref.at[c], part_ref.at[c, low_mine], across_ref.at[c])

    loads[0].wait()
    pl.loop(3, 6)(partial)
    greeted(10)
    for zone in range(2):
        ring_send(zone, 0, 0)
        ring_send(zone, 1, 1)
    share_send(3, 6)
    pl.loop(0, 3)(partial)
    share_send(0, 3)
    pl.loop(6, 8)(partial)
    share_send(6, 8)

    loads[1].wait()

    @pl.loop(0, 8)
    def _(c):
        term = dot(cot_ref[:, block(c, WIDTH)], dest_ref[...], ((0,), (0,))).astype(BF16)
        for i in range(4):
            term_ref[i % 2, lax.rem(2 * c + i // 2, 4), c // 2] = term[i * FEAT : (i + 1) * FEAT]

    swap = remote(term_ref.at[1 - core], core_ref, red_s.at[0], red_r.at[0], sibling, mp)
    swap.start()
    pending.append(swap)
    for zone in range(2):
        ring_take(zone, 0, 0)
        ring_send(zone, 0, 1)
    share_take(0)
    ring_send(2, 1, 0)
    ring_send(2, 0, 1)

    swap.wait_recv()

    @pl.loop(0, 16)
    def _(i):
        ref = term_ref.at[core, i // 4, lax.rem(i, 4)]
        add(ref, ref, core_ref.at[i // 4, lax.rem(i, 4)])

    xcopies = []
    for n, i in enumerate((1, 3, 2)):
        copy = remote(term_ref.at[core, lax.rem(x + i, 4)], xin_ref.at[n], red_s.at[1 + n], red_r.at[1 + n], xs[n], mp)
        copy.start()
        xcopies.append(copy)
    pending.extend(xcopies)
    share_take(1)
    share_take(2)

    def ring_step(zone, way, step):
        ring_take(zone, way, step)
        ring_send(zone, way, step + 1)

    for zone, way in ((0, 1), (1, 1), (0, 0), (1, 0)):
        ring_step(zone, way, 1)
    ring_step(2, 1, 0)
    ring_step(2, 0, 1)
    for zone, way in ((0, 1), (1, 1), (0, 0), (1, 0)):
        ring_step(zone, way, 2)
    ring_step(2, 1, 1)
    ring_step(2, 0, 2)
    ring_step(2, 1, 2)

    for zone in range(2):
        for way in range(2):
            ring_copy(zone, way, 3).wait_recv()
        own = ring_ref_of(zone, 0)
        add(own, own, ring_ref.at[zone, 0, 3], ring_ref.at[zone, 1, 3])
    fold = remote(part_ref.at[0, other], fold_ref, fold_s.at[3], fold_r.at[3], dp, across)
    fold.start()
    for way in range(2):
        ring_copy(2, way, 3).wait_recv()
    add(att_ref.at[0, low_mine], half_ref.at[0], ring_ref.at[2, 0, 3], ring_ref.at[2, 1, 3])

    def low_copy(rows):
        return remote(att_ref.at[0, rows], att_ref.at[0, rows], fold_s.at[4], fold_r.at[4], dp, across)

    low_copy(low_mine).start()
    pending.extend([fold, low_copy(low_mine)])

    def att_copy(part, c):
        rows, cols = pl.ds(part * SUB, SUB), block(lax.rem(y + c, 8), WIDTH)
        return pltpu.make_async_copy(att_ref.at[c, rows], att_hbm.at[rows, cols], att_store.at[part, c])

    def gather_copy(zone, way, step):
        rows = mine if zone == 2 else pl.ds(SUB + 64 * zone, 64)
        src, dst = ((8 - step) % 8, 7 - step) if way == 0 else (step, step + 1)
        sem = (zone, way, step)
        return remote(
            att_ref.at[src, rows], att_ref.at[dst, rows], gath_s.at[sem], gath_r.at[sem], dp, (up, down)[way]
        )

    def gather_send(zone, way, step):
        copy = gather_copy(zone, way, step)
        copy.start()
        pending.append(copy)

    def pass_copy(c, rows):
        return remote(att_ref.at[c, rows], att_ref.at[c, rows], pass_s.at[c], pass_r.at[c], dp, across)

    def gather_take(zone, way, step):
        gather_copy(zone, way, step).wait_recv()
        c = 7 - step if way == 0 else step + 1
        if zone == 2:
            pass_copy(c, mine).start()
        elif zone == 1:
            att_copy(1, c).start()

    fold.wait_recv()
    add(att_ref.at[0, mine], part_ref.at[0, mine], fold_ref)
    gather_send(2, 0, 0)
    gather_send(2, 1, 0)
    pass_copy(0, mine).start()
    low_copy(low_other).wait_recv()
    for zone in range(2):
        gather_send(zone, 0, 0)
        gather_send(zone, 1, 0)
    att_copy(1, 0).start()

    for copy in loads[2:]:
        copy.wait()
    pick_rows(rows_ref, qkv_ref, home)

    @pl.loop(0, 6)
    def _(i):
        slot, cols = i % 2, block(i // 2, HD)
        q, k, v = rows_ref[0, slot, :, cols], rows_ref[1, slot, :, cols], rows_ref[2, slot, :, cols]
        gm = turned_ref[2 + slot, :, cols]
        probs = probabilities(q, k, either(slot, home)[1])
        gp = dot(gm, v, ((1,), (1,)))
        inner = jnp.sum(gp * probs, axis=-1, keepdims=True)
        gs = (probs * (gp - inner) * SCALE).astype(BF16)
        rows_ref[0, slot, :, cols] = dot(gs, k, ((1,), (0,))).astype(BF16)
        rows_ref[1, slot, :, cols] = dot(gs, q, ((0,), (0,))).astype(BF16)
        rows_ref[2, slot, :, cols] = dot(probs.astype(BF16), gm, ((0,), (0,))).astype(BF16)

    outs = []
    for zone, way in ((2, 0), (2, 1), (0, 0), (0, 1), (1, 0), (1, 1)):
        gather_take(zone, way, 0)
        gather_send(zone, way, 1)
    for copy in xcopies:
        copy.wait_recv()

    @pl.loop(0, 4)
    def _(i):
        add(term_ref.at[core, x, i], term_ref.at[core, x, i], *[xin_ref.at[n, i] for n in range(3)])

    zcopies = []
    for n, i in enumerate((1, 3, 2)):
        copy = remote(
            term_ref.at[core, x, lax.rem(zh + i, 4)], zin_ref.at[n], red_s.at[4 + n], red_r.at[4 + n], zs[n], mp
        )
        copy.start()
        zcopies.append(copy)
    pending.extend(zcopies)

    @pl.loop(0, 3)
    def _(i):
        place_rows(grads_ref.at[i], [rows_ref.at[i, 0], rows_ref.at[i, 1]], home)

    for i, ref in enumerate((gq_hbm, gk_hbm, gv_hbm)):
        outs.append(pltpu.make_async_copy(grads_ref.at[i], ref, store.at[i]))
    for copy in outs:
        copy.start()
    for zone, way in ((2, 0), (2, 1), (0, 0), (0, 1), (1, 0), (1, 1)):
        gather_take(zone, way, 1)
        gather_send(zone, way, 2)
    for zone, way in ((2, 0), (2, 1), (0, 0), (0, 1), (1, 0), (1, 1)):
        gather_take(zone, way, 2)
        if way == zone // 2:
            gather_send(zone, way, 3)
    for copy in zcopies:
        copy.wait_recv()
    add(gw_ref, term_ref.at[core, x, zh], *[zin_ref.at[n] for n in range(3)])
    outs.append(pltpu.make_async_copy(gw_ref, gw_hbm, store.at[3]))
    outs[-1].start()
    for zone in (2, 0, 1):
        gather_take(zone, zone // 2, 3)

    @pl.loop(0, 8)
    def _(c):
        pass_copy(c, other).wait_recv()
        att_copy(0, c).start()

    for copy in outs:
        copy.wait()

    @pl.loop(0, 8)
    def _(c):
        att_copy(0, c).wait()
        att_copy(1, c).wait()
        pass_copy(c, mine).wait_send()

    for copy in pending:
        copy.wait_send()


def sds(*shape):
    return jax.ShapeDtypeStruct(shape, BF16)


def buf(*shape):
    return pltpu.VMEM(shape, BF16)


DMA = pltpu.SemaphoreType.DMA


def local(queries, key_rows, value_rows, cotangent, out_weight, patch_counts, destinations):
    smem, hbm, vmem = [pl.BlockSpec(memory_space=space) for space in (pltpu.SMEM, pltpu.HBM, pltpu.VMEM)]
    counts, dests = patch_counts.T, destinations.T
    slots, wt = pl.pallas_call(
        gather_kernel,
        out_shape=(sds(4, SLOT, WIDTH), sds(NDP, FEAT, WIDTH)),
        in_specs=[smem, smem] + [hbm] * 5,
        out_specs=(vmem, hbm),
        scratch_shapes=[
            buf(3, ROWS, WIDTH), buf(DEST, OUT), buf(NDP, FEAT, WIDTH), buf(3, 2, SLOT, WIDTH),
            pltpu.VMEM((DEST, WIDTH), F32), DMA((5,)), DMA((1,)), DMA((31,)), DMA((NDP,)),
        ],
        compiler_params=pltpu.CompilerParams(collective_id=0, has_side_effects=True, vmem_limit_bytes=32 << 20),
        name="gather_forward",
    )(counts, dests, queries, key_rows, value_rows, cotangent, out_weight.T)

    def branch(turn):
        return pl.pallas_call(
            functools.partial(turn_kernel, turn),
            out_shape=sds(4, SLOT, WIDTH),
            in_specs=[vmem],
            out_specs=vmem,
            scratch_shapes=[DMA((4,)), DMA((4,))],
            compiler_params=pltpu.CompilerParams(collective_id=2 + turn, has_side_effects=True),
            name="turn_%d" % turn,
        )

    first = -destinations[0, 0] & (NDP - 1)
    index = jnp.minimum(first, NDP - 1 - first)
    turned = lax.switch(index, [branch(turn) for turn in range(NDP // 2)], slots)

    *outs, grad_weight = pl.pallas_call(
        main_kernel,
        out_shape=(sds(DEST, OUT), sds(ROWS, WIDTH), sds(ROWS, WIDTH), sds(ROWS, WIDTH), sds(FEAT, WIDTH)),
        in_specs=[smem, smem, vmem] + [hbm] * 5,
        out_specs=(hbm,) * 5,
        scratch_shapes=[
            buf(3, ROWS, WIDTH), buf(DEST, OUT), buf(NDP, FEAT, WIDTH), buf(3, 2, SLOT, WIDTH), buf(DEST, WIDTH),
            buf(8, DEST, WIDTH), buf(3, 2, 4, 64, WIDTH), buf(8, 64, WIDTH), buf(8, 64, WIDTH), buf(64, WIDTH),
            buf(8, DEST, WIDTH), buf(2, 4, 4, FEAT, WIDTH), buf(4, 4, FEAT, WIDTH), buf(3, 4, FEAT, WIDTH),
            buf(3, FEAT, WIDTH), buf(3, ROWS, WIDTH), buf(FEAT, WIDTH),
            DMA((5,)), DMA((4,)), DMA((2, 8)), DMA((3, 2, 4)), DMA((3, 2, 4)), DMA((5,)), DMA((5,)),
            DMA((3, 2, 4)), DMA((3, 2, 4)), DMA((8,)), DMA((8,)), DMA((7,)), DMA((7,)),
        ],
        compiler_params=pltpu.CompilerParams(collective_id=1, has_side_effects=True, vmem_limit_bytes=40 << 20),
        name="project_backward",
    )(counts, dests, turned, queries, key_rows, value_rows, cotangent, wt)
    return (*outs, grad_weight.T)


def solution(mesh):
    in_specs = (P("dp", "mp"), P("dp", "mp"), P("dp", "mp"), P("dp", None), P("mp", "dp"), P(), P())
    out_specs = (P("dp", None), P("dp", "mp"), P("dp", "mp"), P("dp", "mp"), P("mp", "dp"))
    return jax.shard_map(local, mesh=mesh, in_specs=in_specs, out_specs=out_specs, check_vma=False)
```

time: 136 us -> 129 us (0.949)
  the two profiles are of different devices: /device:TPU:80 before, /device:TPU:12 now
where the time goes in v1:
time: 129 us; the launch traced here: 128 us
  Pallas kernels  112 us (87%)
  local copies, waits for them, and re-layouts  14.6 us (11%)
  between operations  1.41 us (1%)
    pallas_call x1, Pallas kernels, local(): pl.pallas_call(main_kernel, out_shape=(sds(DEST, OUT), sds(ROWS, WIDTH),...  69.1 us
    pallas_call x1, Pallas kernels, local(): pl.pallas_call(gather_kernel, out_shape=(sds(4, SLOT, WIDTH), sds(NDP, FE...  28.6 us
    pallas_call x1, Pallas kernels, local(): lax.switch(index, [branch(turn) for turn in range(NDP // 2)], slots)  14.7 us
    unnamed x35, local copies, waits for them, and re-layouts  13.4 us

profile of v1, /device:TPU:12, one launch (start us, length us, event | category | flops | bytes accessed | tf_op | source)
XLA Modules:
  0.0 128.4 jit_solution(13614251430876658568)
XLA Ops:
  0.6 1.2 slice.3
  2.5 0.0 copy-start
  2.5 1.4 %copy-done = bf16[256,3072]{1,0:T(8,128)(2,1)S(1)} copy-done((bf16[256,3072]{1,0:T(8,128)(2,1)S(1)}, bf16[256,3072]{1,0:T(8,128)(2,1)}, u32[]{:S(2)}) %copy-start) | copy-done | bytes 1572888
  3.9 0.0 copy-start.4
  3.9 0.9 copy-done.4
  4.8 0.0 copy-start.6
  4.8 0.9 copy-done.6
  5.8 0.0 copy-start.8
  5.8 0.9 copy-done.8
  6.7 0.0 copy-start.10
  6.7 0.9 copy-done.10
  7.6 0.0 copy-start.11
  7.6 0.7 copy-done.11
  8.3 0.0 copy-start.13
  8.3 0.7 copy-done.13
  9.0 28.6 %gather_forward.1 = (bf16[4,160,384]{2,1,0:T(8,128)(2,1)S(1)}, bf16[32,96,384]{2,1,0:T(8,128)(2,1)S(1)}) custom-call(s32[2,32]{1,0:T(2,128)S(1)} %bitcast.7, s32[2,32]{1,0:T(2,128)S(1)} %bitcast.9, bf16[320,384]{1,0:T(8,128)(2,1)S(1)} %copy-done.4, bf16[320,384]{1,0:T(8,128)(2,1)S(1)} %copy-done.6, bf16[320,384]{1,0:T(8,128)(2,1)S(1)} %copy-done.8, ...), custom_call_target="tpu_custom_call" | custom-call | tf_op jit(solution)/shard_map/gather_forward/pallas_call | solution.py:504
  37.5 0.0 copy-start.2
  37.6 1.4 %copy-done.2 = bf16[32,96,384]{2,1,0:T(8,128)(2,1)} copy-done((bf16[32,96,384]{2,1,0:T(8,128)(2,1)}, bf16[32,96,384]{2,1,0:T(8,128)(2,1)S(1)}, u32[]{:S(2)}) %copy-start.2) | copy-done | bytes 2359320
  39.0 0.0 copy-start.1
  39.0 0.0 copy-start.5
  39.0 0.0 copy-start.7
  39.0 0.0 copy-start.9
  39.0 0.0 copy-start.12
  39.0 0.0 copy-start.14
  39.0 14.7 %conditional.1 = (bf16[4,160,384]{2,1,0:T(8,128)(2,1)S(1)}) conditional(s32[]{:T(128)} %clamp.3, bf16[4,160,384]{2,1,0:T(8,128)(2,1)S(1)} %get-tuple-element.45, bf16[4,160,384]{2,1,0:T(8,128)(2,1)S(1)} %get-tuple-element.45, bf16[4,160,384]{2,1,0:T(8,128)(2,1)S(1)} %get-tuple-element.45, ...), branch_computations={%region_0.0_spmd, %region_1.0_spmd, %region_2.0_spmd, %region_3.0_... | conditional | bytes 8 | solution.py:530
  39.1 14.7 %turn_9.1 = bf16[4,160,384]{2,1,0:T(8,128)(2,1)S(1)} custom-call(bf16[4,160,384]{2,1,0:T(8,128)(2,1)S(1)} %in_ref.9), custom_call_target="tpu_custom_call" | custom-call | tf_op jit(solution)/shard_map/cond/branch_9_fun/turn_9/pallas_call | solution.py:530
  53.8 0.0 copy-done.1
  53.8 0.0 copy-done.5
  53.8 0.0 copy-done.7
  53.8 0.0 copy-done.9
  53.8 0.0 copy-done.12
  53.8 0.0 copy-done.14
  53.8 0.0 copy-start.3
  53.8 1.7 %copy-done.3 = bf16[32,96,384]{2,1,0:T(8,128)(2,1)S(1)} copy-done((bf16[32,96,384]{2,1,0:T(8,128)(2,1)S(1)}, bf16[32,96,384]{2,1,0:T(8,128)(2,1)}, u32[]{:S(2)}) %copy-start.3) | copy-done | bytes 2359320
  55.5 69.1 %project_backward.1 = (bf16[256,3072]{1,0:T(8,128)(2,1)S(1)}, bf16[320,384]{1,0:T(8,128)(2,1)S(1)}, bf16[320,384]{1,0:T(8,128)(2,1)S(1)}, bf16[320,384]{1,0:T(8,128)(2,1)S(1)}, bf16[96,384]{1,0:T(8,128)(2,1)S(1)}) custom-call(s32[2,32]{1,0:T(2,128)S(1)} %bitcast.8, s32[2,32]{1,0:T(2,128)S(1)} %bitcast.10, ...), custom_call_target="tpu_custom_call" | custom-call | tf_op jit(solution)/shard_map/project_backward/pallas_call | solution.py:532
  124.5 1.1 copy.33
  125.7 0.7 copy.34
  126.4 0.7 copy.35
  127.1 0.7 copy.36
  127.8 0.6 copy.37
Async XLA Ops:
  2.5 1.4 %copy-start = (bf16[256,3072]{1,0:T(8,128)(2,1)S(1)}, bf16[256,3072]{1,0:T(8,128)(2,1)}, u32[]{:S(2)}) copy-start(bf16[256,3072]{1,0:T(8,128)(2,1)} %cot_hbm.3) | copy-start | bytes 4718596
  3.9 0.9 copy-start.4
  4.8 0.9 copy-start.6
  5.8 0.9 copy-start.8
  6.7 0.9 copy-start.10
  7.6 0.7 copy-start.11
  8.3 0.7 copy-start.13
  37.5 1.4 %copy-start.2 = (bf16[32,96,384]{2,1,0:T(8,128)(2,1)}, bf16[32,96,384]{2,1,0:T(8,128)(2,1)S(1)}, u32[]{:S(2)}) copy-start(bf16[32,96,384]{2,1,0:T(8,128)(2,1)S(1)} %get-tuple-element.46.wt_hbm) | copy-start | bytes 7077892
  39.0 14.8 %copy-start.1 = (bf16[256,3072]{1,0:T(8,128)(2,1)S(1)}, bf16[256,3072]{1,0:T(8,128)(2,1)}, u32[]{:S(2)}) copy-start(bf16[256,3072]{1,0:T(8,128)(2,1)} %cot_hbm.3) | copy-start | bytes 4718596
  39.0 14.8 %copy-start.5 = (bf16[320,384]{1,0:T(8,128)(2,1)S(1)}, bf16[320,384]{1,0:T(8,128)(2,1)}, u32[]{:S(2)}) copy-start(bf16[320,384]{1,0:T(8,128)(2,1)} %q_hbm.3) | copy-start | bytes 737284
  39.0 14.8 %copy-start.7 = (bf16[320,384]{1,0:T(8,128)(2,1)S(1)}, bf16[320,384]{1,0:T(8,128)(2,1)}, u32[]{:S(2)}) copy-start(bf16[320,384]{1,0:T(8,128)(2,1)} %k_hbm.3) | copy-start | bytes 737284
  39.0 14.8 %copy-start.9 = (bf16[320,384]{1,0:T(8,128)(2,1)S(1)}, bf16[320,384]{1,0:T(8,128)(2,1)}, u32[]{:S(2)}) copy-start(bf16[320,384]{1,0:T(8,128)(2,1)} %v_hbm.3) | copy-start | bytes 737284
  39.0 14.8 %copy-start.12 = (s32[32,2]{0,1:T(2,128)S(1)}, s32[32,2]{0,1:T(2,128)}, u32[]{:S(2)}) copy-start(s32[32,2]{0,1:T(2,128)} %param.28) | copy-start | bytes 772
  39.0 14.8 %copy-start.14 = (s32[32,2]{0,1:T(2,128)S(1)}, s32[32,2]{0,1:T(2,128)}, u32[]{:S(2)}) copy-start(s32[32,2]{0,1:T(2,128)} %param.29) | copy-start | bytes 772
  53.8 1.7 %copy-start.3 = (bf16[32,96,384]{2,1,0:T(8,128)(2,1)S(1)}, bf16[32,96,384]{2,1,0:T(8,128)(2,1)}, u32[]{:S(2)}) copy-start(bf16[32,96,384]{2,1,0:T(8,128)(2,1)} %copy-done.2) | copy-start | bytes 7077892
